TPU v7x, 32 devices: a whole 2x2x4 slice. The times are simulated.
32 devices in a mesh: query: 2 (over x), gallery: 16 (over z, y, core).
Axes of the slice: x: 2, y: 2, z: 4, core: 2. Of those that a mesh axis runs over, the one named last changes fastest.
Arguments:
- query_hidden: bfloat16 [768, 32, 768], P(('query', 'gallery')), may hold values from -6 to 6
- query_mask: int32 [768, 32], P(('query', 'gallery')), may hold values 0 or 1
- passage_hidden: bfloat16 [16, 360, 768], P('gallery', 'query'), may hold values from -6 to 6
- passage_ids: int32 [16, 360], P('gallery', 'query'), may hold values from 999 to 30521, as said below
- passage_lengths: int32 [32], P('gallery'), may hold values from 30 to 180, as said below
- projection: bfloat16 [768, 128], replicated, may hold values from -0.21875 to 0.21875
Outputs:
- scores: float32 [768, 32], P(('query', 'gallery'))
Inputs may be any that keep to these rules, and one draw needn't show every extreme that they name: `passage_ids`: ids from 999 to 1066 are punctuation; the rest are words. `passage_lengths`: some passage has exactly 180 tokens.
All inputs are finite; a program needn't handle non-finite values. No bound on the sum of `query_mask` on one device may be relied on, other than what follows from the above.
Results may differ from a plain program's by a relative error of at most 0.00036.
Values may be sent and summed in bfloat16 or wider, within the bound.
A program may use at most 64 MiB of HBM per device.

v0:
```python
import math
import jax
import jax.numpy as jnp
from jax import lax
from jax.sharding import PartitionSpec as P

DIM = 128
PLEN = 180
QLEN = 32
PUNCT_LO = 999
PUNCT_HI = 1067
PASS_GRP = 2
EPS = 1e-06
NEG = -1000000000.0


def unit_rows(hidden, projection):
    flat_rows = hidden.reshape(-1, hidden.shape[-1])
    projected = jnp.dot(flat_rows, projection, preferred_element_type=jnp.float32)
    inverse_norm = lax.rsqrt(jnp.sum(projected * projected, axis=-1, keepdims=True) + EPS)
    return (projected * inverse_norm).astype(jnp.bfloat16)


def local(query_hidden, query_mask, passage_hidden, passage_ids, passage_lengths, projection):
    row_count = passage_hidden.shape[1]
    query_count = query_hidden.shape[0]
    groups = lax.axis_size("gallery")
    query_block = lax.axis_index("query")
    position = query_block * row_count + jnp.arange(row_count, dtype=jnp.int32)
    passage_slot = position // PLEN
    token_pos = position % PLEN
    onehot = passage_slot[:, None] == jnp.arange(PASS_GRP, dtype=jnp.int32)[None, :]
    length_rows = jnp.sum(jnp.where(onehot, passage_lengths[None, :], 0), axis=1)
    token_ids = passage_ids[0]
    punctuation = (token_ids >= PUNCT_LO) & (token_ids < PUNCT_HI)
    kept = (token_pos < length_rows) & ((token_pos == 0) | jnp.logical_not(punctuation))
    kept_flag = kept.astype(jnp.bfloat16)[None, :]
    passage_unit = unit_rows(passage_hidden, projection).reshape(1, row_count, DIM)
    query_unit = unit_rows(query_hidden, projection)
    weights = query_mask.astype(jnp.float32).reshape(-1)
    thin_units, thin_flags = (
        lax.all_gather(passage_unit, "gallery", axis=0, tiled=True),
        lax.all_gather(kept_flag, "gallery", axis=0, tiled=True),
    )
    initial = jnp.full((query_unit.shape[0], groups * PASS_GRP), NEG, jnp.float32)
    piece_units = lax.all_gather(thin_units, "query", axis=1, tiled=True)
    piece_flags = lax.all_gather(thin_flags, "query", axis=1, tiled=True)
    piece_rows = piece_units.shape[1]
    row_slot = jnp.arange(piece_rows, dtype=jnp.int32) // PLEN
    block_width = math.gcd(groups, 4)
    unit_blocks = piece_units.reshape(groups // block_width, block_width * piece_rows, DIM)
    flag_blocks = piece_flags.reshape(groups // block_width, 1, block_width * piece_rows)

    def one_block(block_pair):
        unit_block, flag_block = block_pair
        similar = jnp.einsum(
            "td,rd->tr", query_unit, unit_block, preferred_element_type=jnp.float32
        )
        similar = jnp.where(flag_block > 0, similar, NEG).reshape(-1, block_width, piece_rows)
        per_member = [
            jnp.max(jnp.where(row_slot == member, similar, NEG), axis=2)
            for member in range(PASS_GRP)
        ]
        return jnp.stack(per_member, axis=2)

    fresh_max = lax.map(one_block, (unit_blocks, flag_blocks))
    fresh_max = jnp.transpose(fresh_max, (1, 0, 2, 3)).reshape(initial.shape)
    running = jnp.maximum(initial, fresh_max)
    scores = jnp.sum(
        (running * weights[:, None]).reshape(query_count, QLEN, groups * PASS_GRP), axis=1
    )
    return scores


def solution(mesh):
    placed = (
        P(("query", "gallery"), None, None),
        P(("query", "gallery"), None),
        P("gallery", "query", None),
        P("gallery", "query"),
        P("gallery"),
        P(),
    )
    return jax.shard_map(
        local, mesh=mesh, in_specs=placed, out_specs=P(("query", "gallery"), None), check_vma=False
    )
```

profile of v0, /device:TPU:0, one launch (start us, length us, event | category | flops | bytes accessed | tf_op | source)
XLA Modules:
  0.0 77.6 jit_solution(7608371529911874838)
XLA Ops:
  6.5 1.4 %multiply_reduce_fusion.2 = (f32[180]{0:T(256)S(1)}, f32[180,128]{1,0:T(8,128)S(1)}) fusion(bf16[768,128]{1,0:T(8,128)(2,1)} %param.13, bf16[1,180,768]{2,1,0:T(8,128)(2,1)} %param.10), kind=kOutput, calls=%fused_computation.26 | convolution fusion | flops 35435340 | bytes 565968 | tf_op jit(solution)/shard_map/dot_general | solution.py:19
  8.0 0.1 fusion.11
  8.1 0.0 copy-start.1
  8.1 25.5 %all-gather.3 = bf16[16,180,128]{2,1,0:T(8,128)(2,1)S(1)} all-gather(bf16[1,180,128]{2,1,0:T(8,128)(2,1)S(1)} %fusion.11), channel_id=2, replica_groups=mesh['query'=2,'gallery'=16] {'gallery'}, dimensions={0}, use_global_device_ids=true | all-gather | bytes 783360 | tf_op jit(solution)/shard_map/all_gather | solution.py:42
  33.6 1.0 %copy.25 = bf16[16,180,128]{2,0,1:T(8,128)(2,1)} copy(bf16[16,180,128]{2,1,0:T(8,128)(2,1)S(1)} %all-gather.3) | data formatting | bytes 1474560 | tf_op jit(solution)/shard_map/all_gather | solution.py:42
  34.6 0.0 all-gather.6.cloned.1.call-update
  34.6 0.0 copy-start.4
  34.6 0.0 copy-start.3
  34.7 0.0 copy-done
  34.7 0.0 copy-start.2
  34.7 0.6 multiply_reduce_fusion.1
  35.3 0.2 copy.28
  35.5 0.1 fusion.12
  35.6 17.5 %all-gather.1 = bf16[16,1,180]{2,1,0:T(2,128)(2,1)S(1)} all-gather(bf16[1,1,180]{2,1,0:T(2,128)(2,1)S(1)} %fusion.13), channel_id=1, replica_groups=mesh['query'=2,'gallery'=16] {'gallery'}, dimensions={0}, use_global_device_ids=true | all-gather | bytes 6120 | tf_op jit(solution)/shard_map/all_gather | solution.py:43
  53.1 4.5 %all-gather.2 = bf16[2,180,16]{1,2,0:T(8,128)(2,1)S(1)} all-gather(bf16[1,180,16]{1,2,0:T(8,128)(2,1)S(1)} %bitcast.56), channel_id=1, replica_groups=mesh['query'=2,'gallery'=16] {'query'}, dimensions={0}, use_global_device_ids=true | all-gather | bytes 17280 | tf_op jit(solution)/shard_map/all_gather | solution.py:47
  57.6 0.1 reshape.108
  57.7 0.1 reshape.113
  57.8 0.5 all-gather.6.cloned.1.call-done
  58.3 1.8 %copy.26 = bf16[16,360,128]{2,1,0:T(8,128)(2,1)S(1)} copy(bf16[16,360,128]{2,0,1:T(8,128)(2,1)} %all-gather.6.cloned.1.call-done) | data formatting | bytes 2949120 | tf_op jit(solution)/shard_map/all_gather | solution.py:46
  60.1 9.6 %while.12 = (s32[]{:T(128)}, f32[4,768,4,2]{1,3,2,0:T(2,128)S(1)}, bf16[4,1,1440]{2,1,0:T(2,128)(2,1)S(1)}, bf16[4,1440,128]{2,1,0:T(8,128)(2,1)S(1)}, bf16[768,128]{1,0:T(8,128)(2,1)S(1)}, /*index=5*/s32[]{:T(128)}) while((s32[]{:T(128)}, f32[4,768,4,2]{1,3,2,0:T(2,128)S(1)}, bf16[4,1,1440]{2,1,0:T(2,128)(2,1)S(1)}, ...), condition=%wide.region_6.7_spmd.clone.clone, body=%wide.region_3.6_spmd.clone.clone.sunk | while | flops 288650176 | bytes 9543377 | solution.py:66
  60.2 1.1 %convolution_select_fusion.2 = f32[1440,768]{1,0:T(8,128)S(1)} fusion(bf16[768,128]{1,0:T(8,128)(2,1)S(1)} %get-tuple-element.172, pred[1440]{0:T(1024)(128)(4,1)S(1)} %compare_reduce_fusion.2, bf16[4,1440,128]{2,1,0:T(8,128)(2,1)S(1)} %get-tuple-element.171, s32[]{:T(128)} %get-tuple-element.162), kind=kOutput, calls=%fused_computation.3.clone.1 | convolution fusion | flops 284221440 | bytes 4990980 | tf_op jit(solution)/shard_map/while/body/eval_jaxpr/td,rd->tr/dot_general | solution.py:56
  61.3 1.1 %select_reduce_fusion.3 = (f32[768,4]{0,1:T(4,128)S(1)}, f32[768,4]{0,1:T(4,128)S(1)}) fusion(f32[768,4,360]{0,2,1:T(8,128)S(1)} %bitcast.53, pred[360]{0:T(512)(128)(4,1)S(1)} %get-tuple-element.152, pred[360]{0:T(512)(128)(4,1)S(1)} %get-tuple-element.153), kind=kLoop, calls=%fused_computation.2.clone.1 | loop fusion | flops 4417536 | bytes 4448976 | tf_op jit(solution)/shard_map/while/body/eval_jaxpr/reduce_max | solution.py:61
  62.5 1.1 %convolution_select_fusion.2 = f32[1440,768]{1,0:T(8,128)S(1)} fusion(bf16[768,128]{1,0:T(8,128)(2,1)S(1)} %get-tuple-element.172, pred[1440]{0:T(1024)(128)(4,1)S(1)} %compare_reduce_fusion.2, bf16[4,1440,128]{2,1,0:T(8,128)(2,1)S(1)} %get-tuple-element.171, s32[]{:T(128)} %get-tuple-element.162), kind=kOutput, calls=%fused_computation.3.clone.1 | convolution fusion | flops 284221440 | bytes 4990980 | tf_op jit(solution)/shard_map/while/body/eval_jaxpr/td,rd->tr/dot_general | solution.py:56
  63.7 1.1 %select_reduce_fusion.3 = (f32[768,4]{0,1:T(4,128)S(1)}, f32[768,4]{0,1:T(4,128)S(1)}) fusion(f32[768,4,360]{0,2,1:T(8,128)S(1)} %bitcast.53, pred[360]{0:T(512)(128)(4,1)S(1)} %get-tuple-element.152, pred[360]{0:T(512)(128)(4,1)S(1)} %get-tuple-element.153), kind=kLoop, calls=%fused_computation.2.clone.1 | loop fusion | flops 4417536 | bytes 4448976 | tf_op jit(solution)/shard_map/while/body/eval_jaxpr/reduce_max | solution.py:61
  64.9 1.1 %convolution_select_fusion.2 = f32[1440,768]{1,0:T(8,128)S(1)} fusion(bf16[768,128]{1,0:T(8,128)(2,1)S(1)} %get-tuple-element.172, pred[1440]{0:T(1024)(128)(4,1)S(1)} %compare_reduce_fusion.2, bf16[4,1440,128]{2,1,0:T(8,128)(2,1)S(1)} %get-tuple-element.171, s32[]{:T(128)} %get-tuple-element.162), kind=kOutput, calls=%fused_computation.3.clone.1 | convolution fusion | flops 284221440 | bytes 4990980 | tf_op jit(solution)/shard_map/while/body/eval_jaxpr/td,rd->tr/dot_general | solution.py:56
  66.1 1.1 %select_reduce_fusion.3 = (f32[768,4]{0,1:T(4,128)S(1)}, f32[768,4]{0,1:T(4,128)S(1)}) fusion(f32[768,4,360]{0,2,1:T(8,128)S(1)} %bitcast.53, pred[360]{0:T(512)(128)(4,1)S(1)} %get-tuple-element.152, pred[360]{0:T(512)(128)(4,1)S(1)} %get-tuple-element.153), kind=kLoop, calls=%fused_computation.2.clone.1 | loop fusion | flops 4417536 | bytes 4448976 | tf_op jit(solution)/shard_map/while/body/eval_jaxpr/reduce_max | solution.py:61
  67.3 1.1 %convolution_select_fusion.2 = f32[1440,768]{1,0:T(8,128)S(1)} fusion(bf16[768,128]{1,0:T(8,128)(2,1)S(1)} %get-tuple-element.172, pred[1440]{0:T(1024)(128)(4,1)S(1)} %compare_reduce_fusion.2, bf16[4,1440,128]{2,1,0:T(8,128)(2,1)S(1)} %get-tuple-element.171, s32[]{:T(128)} %get-tuple-element.162), kind=kOutput, calls=%fused_computation.3.clone.1 | convolution fusion | flops 284221440 | bytes 4990980 | tf_op jit(solution)/shard_map/while/body/eval_jaxpr/td,rd->tr/dot_general | solution.py:56
  68.5 1.1 %select_reduce_fusion.3 = (f32[768,4]{0,1:T(4,128)S(1)}, f32[768,4]{0,1:T(4,128)S(1)}) fusion(f32[768,4,360]{0,2,1:T(8,128)S(1)} %bitcast.53, pred[360]{0:T(512)(128)(4,1)S(1)} %get-tuple-element.152, pred[360]{0:T(512)(128)(4,1)S(1)} %get-tuple-element.153), kind=kLoop, calls=%fused_computation.2.clone.1 | loop fusion | flops 4417536 | bytes 4448976 | tf_op jit(solution)/shard_map/while/body/eval_jaxpr/reduce_max | solution.py:61
  69.7 0.1 maximum_bitcast_fusion.1
  69.7 0.2 max_broadcast_in_dim.12
  69.9 0.2 multiply_reduce_fusion
  70.1 0.7 copy.29
  (35 shorter events, 0.6 us)
Async XLA Ops:
  6.5 28.1 %copy-start = (bf16[24,32,768]{2,1,0:T(8,128)(2,1)S(1)}, bf16[24,32,768]{2,1,0:T(8,128)(2,1)}, u32[]{:S(2)}) copy-start(bf16[24,32,768]{2,1,0:T(8,128)(2,1)} %param.8) | copy-start | bytes 3538948
  6.5 51.8 %all-gather.6.cloned.1.call-start = ((), (), s32[]{:S(2)}) async-start(), calls=%async_computation | async-start | bytes 2211840 | tf_op jit(solution)/shard_map/all_gather | solution.py:46
  8.1 26.6 %copy-start.1 = (bf16[768,128]{1,0:T(8,128)(2,1)S(1)}, bf16[768,128]{1,0:T(8,128)(2,1)}, u32[]{:S(2)}) copy-start(bf16[768,128]{1,0:T(8,128)(2,1)} %param.13) | copy-start | bytes 589828
  34.6 0.9 %copy-start.4 = (s32[2]{0:T(128)S(1)}, s32[2]{0:T(128)}, u32[]{:S(2)}) copy-start(s32[2]{0:T(128)} %param.12) | copy-start | bytes 28
  34.6 1.0 %copy-start.3 = (s32[1,180]{1,0:T(1,128)S(1)}, s32[1,180]{1,0:T(1,128)}, u32[]{:S(2)}) copy-start(s32[1,180]{1,0:T(1,128)} %param.11) | copy-start | bytes 2164
  34.7 23.1 %copy-start.2 = (s32[24,32]{1,0:T(8,128)S(1)}, s32[24,32]{1,0:T(8,128)}, u32[]{:S(2)}) copy-start(s32[24,32]{1,0:T(8,128)} %param.9) | copy-start | bytes 9220
Sparse Core Ops, SparseCore 0:
  34.7 23.5 all-gather.5
where the time goes:
time: 77.8 us; the launch traced here: 77.6 us
  blocking collectives  47.5 us (61%)
  between operations  13.6 us (17%)
  matrix products  6.51 us (8%)
  other arithmetic  5.26 us (7%)
  local copies, waits for them, and re-layouts  4.07 us (5%)
    all_gather x1, blocking collectives, local(): lax.all_gather(passage_unit, 'gallery', axis=0, tiled=True)  25.5 us
    all_gather x1, blocking collectives, local(): lax.all_gather(kept_flag, 'gallery', axis=0, tiled=True)  17.5 us
    dot_general x4, matrix products, one_block(): jnp.einsum('td,rd->tr', query_unit, unit_block, preferred_element_type=jn...  4.52 us
    all_gather x1, blocking collectives, local(): piece_flags = lax.all_gather(thin_flags, 'query', axis=1, tiled=True)  4.49 us
    reduce_max x4, other arithmetic, one_block(): jnp.max(jnp.where(row_slot == member, similar, NEG), axis=2)  4.39 us
    dot_general x2, matrix products, unit_rows(): jnp.dot(flat_rows, projection, preferred_element_type=jnp.float32)  2 us
    all_gather x1, local copies, waits for them, and re-layouts, local(): piece_units = lax.all_gather(thin_units, 'query', axis=1, tiled=True)  1.75 us
  transfers between devices with their start and end apart: 1, of which 1 were waited for; matrix products, arithmetic and copies ran while one was open for 1% of the time, Pallas kernels for 0%

commit v1 on v0

--- a/solution.py
+++ b/solution.py
@@ -12,6 +12,22 @@
 PASS_GRP = 2
 EPS = 1e-06
 NEG = -1000000000.0
+
+
+def collect(x, axis, dim):
+    ways, here, step = (lax.axis_size(axis), lax.axis_index(axis), x.shape[dim])
+    shape = [n * ways if d == dim else n for d, n in enumerate(x.shape)]
+    full = lax.dynamic_update_slice_in_dim(jnp.zeros(shape, x.dtype), x, here * step, axis=dim)
+    going_up = going_down = x
+    for far in range(1, ways // 2 + 1):
+        going_up = lax.ppermute(going_up, axis, [(d, (d + 1) % ways) for d in range(ways)])
+        full = lax.dynamic_update_slice_in_dim(full, going_up, (here - far) % ways * step, axis=dim)
+        if 2 * far < ways:
+            going_down = lax.ppermute(going_down, axis, [(d, (d - 1) % ways) for d in range(ways)])
+            full = lax.dynamic_update_slice_in_dim(
+                full, going_down, (here + far) % ways * step, axis=dim
+            )
+    return full
 
 
 def unit_rows(hidden, projection):
@@ -40,7 +56,7 @@
     weights = query_mask.astype(jnp.float32).reshape(-1)
     thin_units, thin_flags = (
         lax.all_gather(passage_unit, "gallery", axis=0, tiled=True),
-        lax.all_gather(kept_flag, "gallery", axis=0, tiled=True),
+        collect(kept_flag, "gallery", 0),
     )
     initial = jnp.full((query_unit.shape[0], groups * PASS_GRP), NEG, jnp.float32)
     piece_units = lax.all_gather(thin_units, "query", axis=1, tiled=True)

time: 77.8 us -> 104 us (1.34)
  starting transfers between devices: 0.01 us -> 31 us
  blocking collectives: 47.5 us -> 29.7 us
  waiting for transfers between devices: 0.54 us -> 13.3 us
    ppermute x0 -> x15, starting transfers between devices: none -> 31 us  [the longest x7 30.5 us: collect(): lax.ppermute(going_down, axis, [(d, (d - 1) % ways) for d in range(ways)])]
    all_gather x1 -> x0, blocking collectives: 17.5 us -> none  [local(): lax.all_gather(kept_flag, 'gallery', axis=0, tiled=True)]
    ppermute x0 -> x15, waiting for transfers between devices: none -> 13.2 us  [the longest x8 11.9 us: collect(): lax.ppermute(going_up, axis, [(d, (d + 1) % ways) for d in range(ways)])]
  transfers between devices with their start and end apart: 1 -> 16, of which waited for: 1 -> 14; matrix products, arithmetic and copies ran while one was open for 1% -> 2% of each run, Pallas kernels for 0% -> 0%
where the time goes in v1:
time: 104 us
  starting transfers between devices  31 us (30%)
  blocking collectives  29.7 us (29%)
  between operations  13.6 us (13%)
  waiting for transfers between devices  13.3 us (13%)
  matrix products  6.51 us (6%)
  other arithmetic  5.26 us (5%)
  local copies, waits for them, and re-layouts  4.57 us (4%)
    ppermute x7, starting transfers between devices, collect(): lax.ppermute(going_down, axis, [(d, (d - 1) % ways) for d in range(ways)])  30.5 us
    all_gather x1, blocking collectives, local(): lax.all_gather(passage_unit, 'gallery', axis=0, tiled=True)  25.4 us
    ppermute x8, waiting for transfers between devices, collect(): lax.ppermute(going_up, axis, [(d, (d + 1) % ways) for d in range(ways)])  11.9 us
    dot_general x4, matrix products, one_block(): jnp.einsum('td,rd->tr', query_unit, unit_block, preferred_element_type=jn...  4.51 us
    reduce_max x4, other arithmetic, one_block(): jnp.max(jnp.where(row_slot == member, similar, NEG), axis=2)  4.39 us
    all_gather x1, blocking collectives, local(): piece_flags = lax.all_gather(thin_flags, 'query', axis=1, tiled=True)  4.36 us
  transfers between devices with their start and end apart: 16, of which 14 were waited for; matrix products, arithmetic and copies ran while one was open for 2% of the time, Pallas kernels for 0%

profile of v1, /device:TPU:0, one launch (start us, length us, event | category | flops | bytes accessed | tf_op | source)
XLA Modules:
  0.0 104.1 jit_solution(13159822991051044894)
XLA Ops:
  6.5 1.4 %multiply_reduce_fusion.2 = (f32[180]{0:T(256)S(1)}, f32[180,128]{1,0:T(8,128)S(1)}) fusion(bf16[768,128]{1,0:T(8,128)(2,1)} %param.13, bf16[1,180,768]{2,1,0:T(8,128)(2,1)} %param.10), kind=kOutput, calls=%fused_computation.26 | convolution fusion | flops 35435340 | bytes 565968 | tf_op jit(solution)/shard_map/dot_general | solution.py:35
  8.1 25.4 %all-gather.2 = bf16[16,180,128]{2,1,0:T(8,128)(2,1)S(1)} all-gather(bf16[1,180,128]{2,1,0:T(8,128)(2,1)S(1)} %fusion.11), channel_id=2, replica_groups=mesh['query'=2,'gallery'=16] {'gallery'}, dimensions={0}, use_global_device_ids=true | all-gather | bytes 783360 | tf_op jit(solution)/shard_map/all_gather | solution.py:58
  33.5 1.0 copy.25
  34.6 0.4 collective-permute-start
  35.0 4.1 %collective-permute-start.1 = (bf16[1,180]{1,0:T(2,128)(2,1)S(1)}, bf16[1,180]{1,0:T(2,128)(2,1)S(1)}, u32[]{:S(2)}, u32[]{:S(2)}) collective-permute-start(bf16[1,180]{1,0:T(2,128)(2,1)S(1)} %and_convert_fusion), channel_id=1, source_target_pairs={{0,15},{1,0},{2,1},{3,2},{4,3},{5,4},{6,5},{7,6},{8,7},{9,8},{10,9... | collective-permute-start | bytes 1088 | tf_op jit(solution)/shard_map/ppermute | solution.py:26
  39.1 0.6 multiply_reduce_fusion.1
  39.8 0.6 collective-permute-done
  40.6 4.5 %collective-permute-start.3 = (bf16[1,180]{1,0:T(2,128)(2,1)S(1)}, bf16[1,180]{1,0:T(2,128)(2,1)S(1)}, u32[]{:S(2)}, u32[]{:S(2)}) collective-permute-start(bf16[1,180]{1,0:T(2,128)(2,1)S(1)} %collective-permute-done.1), channel_id=1, source_target_pairs={{0,15},{1,0},{2,1},{3,2},{4,3},{5,4},{6,5},{7,6},{8,7},{9,8},{10,9... | collective-permute-start | bytes 1088 | tf_op jit(solution)/shard_map/ppermute | solution.py:26
  45.1 1.0 collective-permute-done.2
  46.4 4.4 %collective-permute-start.5 = (bf16[1,180]{1,0:T(2,128)(2,1)S(1)}, bf16[1,180]{1,0:T(2,128)(2,1)S(1)}, u32[]{:S(2)}, u32[]{:S(2)}) collective-permute-start(bf16[1,180]{1,0:T(2,128)(2,1)S(1)} %collective-permute-done.3), channel_id=1, source_target_pairs={{0,15},{1,0},{2,1},{3,2},{4,3},{5,4},{6,5},{7,6},{8,7},{9,8},{10,9... | collective-permute-start | bytes 1088 | tf_op jit(solution)/shard_map/ppermute | solution.py:26
  50.8 1.0 collective-permute-done.4
  52.1 4.4 %collective-permute-start.7 = (bf16[1,180]{1,0:T(2,128)(2,1)S(1)}, bf16[1,180]{1,0:T(2,128)(2,1)S(1)}, u32[]{:S(2)}, u32[]{:S(2)}) collective-permute-start(bf16[1,180]{1,0:T(2,128)(2,1)S(1)} %collective-permute-done.5), channel_id=1, source_target_pairs={{0,15},{1,0},{2,1},{3,2},{4,3},{5,4},{6,5},{7,6},{8,7},{9,8},{10,9... | collective-permute-start | bytes 1088 | tf_op jit(solution)/shard_map/ppermute | solution.py:26
  56.5 1.0 collective-permute-done.6
  57.8 4.4 %collective-permute-start.9 = (bf16[1,180]{1,0:T(2,128)(2,1)S(1)}, bf16[1,180]{1,0:T(2,128)(2,1)S(1)}, u32[]{:S(2)}, u32[]{:S(2)}) collective-permute-start(bf16[1,180]{1,0:T(2,128)(2,1)S(1)} %collective-permute-done.7), channel_id=1, source_target_pairs={{0,15},{1,0},{2,1},{3,2},{4,3},{5,4},{6,5},{7,6},{8,7},{9,8},{10,9... | collective-permute-start | bytes 1088 | tf_op jit(solution)/shard_map/ppermute | solution.py:26
  62.2 1.0 collective-permute-done.8
  63.5 4.4 %collective-permute-start.11 = (bf16[1,180]{1,0:T(2,128)(2,1)S(1)}, bf16[1,180]{1,0:T(2,128)(2,1)S(1)}, u32[]{:S(2)}, u32[]{:S(2)}) collective-permute-start(bf16[1,180]{1,0:T(2,128)(2,1)S(1)} %collective-permute-done.9), channel_id=1, source_target_pairs={{0,15},{1,0},{2,1},{3,2},{4,3},{5,4},{6,5},{7,6},{8,7},{9,8},{10,9... | collective-permute-start | bytes 1088 | tf_op jit(solution)/shard_map/ppermute | solution.py:26
  67.8 1.0 collective-permute-done.10
  69.1 4.4 %collective-permute-start.13 = (bf16[1,180]{1,0:T(2,128)(2,1)S(1)}, bf16[1,180]{1,0:T(2,128)(2,1)S(1)}, u32[]{:S(2)}, u32[]{:S(2)}) collective-permute-start(bf16[1,180]{1,0:T(2,128)(2,1)S(1)} %collective-permute-done.11), channel_id=1, source_target_pairs={{0,15},{1,0},{2,1},{3,2},{4,3},{5,4},{6,5},{7,6},{8,7},{9,8},{10,9... | collective-permute-start | bytes 1088 | tf_op jit(solution)/shard_map/ppermute | solution.py:26
  73.5 1.0 collective-permute-done.12
  74.9 5.4 %collective-permute-done.14 = bf16[1,180]{1,0:T(2,128)(2,1)S(1)} collective-permute-done((bf16[1,180]{1,0:T(2,128)(2,1)S(1)}, bf16[1,180]{1,0:T(2,128)(2,1)S(1)}, u32[]{:S(2)}, u32[]{:S(2)}) %collective-permute-start.14) | collective-permute-done | bytes 392 | tf_op jit(solution)/shard_map/ppermute | solution.py:23
  80.2 4.4 %all-gather.1 = bf16[2,180,16]{1,2,0:T(8,128)(2,1)S(1)} all-gather(bf16[1,180,16]{1,2,0:T(8,128)(2,1)S(1)} %bitcast.50), channel_id=1, replica_groups=mesh['query'=2,'gallery'=16] {'query'}, dimensions={0}, use_global_device_ids=true | all-gather | bytes 17280 | tf_op jit(solution)/shard_map/all_gather | solution.py:63
  84.8 1.8 %copy.26 = bf16[16,360,128]{2,1,0:T(8,128)(2,1)S(1)} copy(bf16[16,360,128]{2,0,1:T(8,128)(2,1)} %all-gather.5.cloned.1.call-done) | data formatting | bytes 2949120 | tf_op jit(solution)/shard_map/all_gather | solution.py:62
  86.6 9.6 %while.12 = (s32[]{:T(128)}, f32[4,768,4,2]{1,3,2,0:T(2,128)S(1)}, bf16[4,1,1440]{2,1,0:T(2,128)(2,1)S(1)}, bf16[4,1440,128]{2,1,0:T(8,128)(2,1)S(1)}, bf16[768,128]{1,0:T(8,128)(2,1)S(1)}, /*index=5*/s32[]{:T(128)}) while((s32[]{:T(128)}, f32[4,768,4,2]{1,3,2,0:T(2,128)S(1)}, bf16[4,1,1440]{2,1,0:T(2,128)(2,1)S(1)}, ...), condition=%wide.region_6.7_spmd.clone.clone, body=%wide.region_3.6_spmd.clone.clone.sunk | while | flops 288650176 | bytes 9543377 | solution.py:82
  86.6 1.1 %convolution_select_fusion.2 = f32[1440,768]{1,0:T(8,128)S(1)} fusion(bf16[768,128]{1,0:T(8,128)(2,1)S(1)} %get-tuple-element.172, pred[1440]{0:T(1024)(128)(4,1)S(1)} %compare_reduce_fusion.2, bf16[4,1440,128]{2,1,0:T(8,128)(2,1)S(1)} %get-tuple-element.171, s32[]{:T(128)} %get-tuple-element.162), kind=kOutput, calls=%fused_computation.3.clone.1 | convolution fusion | flops 284221440 | bytes 4990980 | tf_op jit(solution)/shard_map/while/body/eval_jaxpr/td,rd->tr/dot_general | solution.py:72
  87.8 1.1 %select_reduce_fusion.3 = (f32[768,4]{0,1:T(4,128)S(1)}, f32[768,4]{0,1:T(4,128)S(1)}) fusion(f32[768,4,360]{0,2,1:T(8,128)S(1)} %bitcast.47, pred[360]{0:T(512)(128)(4,1)S(1)} %get-tuple-element.152, pred[360]{0:T(512)(128)(4,1)S(1)} %get-tuple-element.153), kind=kLoop, calls=%fused_computation.2.clone.1 | loop fusion | flops 4417536 | bytes 4448976 | tf_op jit(solution)/shard_map/while/body/eval_jaxpr/reduce_max | solution.py:77
  89.0 1.1 %convolution_select_fusion.2 = f32[1440,768]{1,0:T(8,128)S(1)} fusion(bf16[768,128]{1,0:T(8,128)(2,1)S(1)} %get-tuple-element.172, pred[1440]{0:T(1024)(128)(4,1)S(1)} %compare_reduce_fusion.2, bf16[4,1440,128]{2,1,0:T(8,128)(2,1)S(1)} %get-tuple-element.171, s32[]{:T(128)} %get-tuple-element.162), kind=kOutput, calls=%fused_computation.3.clone.1 | convolution fusion | flops 284221440 | bytes 4990980 | tf_op jit(solution)/shard_map/while/body/eval_jaxpr/td,rd->tr/dot_general | solution.py:72
  90.2 1.1 %select_reduce_fusion.3 = (f32[768,4]{0,1:T(4,128)S(1)}, f32[768,4]{0,1:T(4,128)S(1)}) fusion(f32[768,4,360]{0,2,1:T(8,128)S(1)} %bitcast.47, pred[360]{0:T(512)(128)(4,1)S(1)} %get-tuple-element.152, pred[360]{0:T(512)(128)(4,1)S(1)} %get-tuple-element.153), kind=kLoop, calls=%fused_computation.2.clone.1 | loop fusion | flops 4417536 | bytes 4448976 | tf_op jit(solution)/shard_map/while/body/eval_jaxpr/reduce_max | solution.py:77
  91.4 1.1 %convolution_select_fusion.2 = f32[1440,768]{1,0:T(8,128)S(1)} fusion(bf16[768,128]{1,0:T(8,128)(2,1)S(1)} %get-tuple-element.172, pred[1440]{0:T(1024)(128)(4,1)S(1)} %compare_reduce_fusion.2, bf16[4,1440,128]{2,1,0:T(8,128)(2,1)S(1)} %get-tuple-element.171, s32[]{:T(128)} %get-tuple-element.162), kind=kOutput, calls=%fused_computation.3.clone.1 | convolution fusion | flops 284221440 | bytes 4990980 | tf_op jit(solution)/shard_map/while/body/eval_jaxpr/td,rd->tr/dot_general | solution.py:72
  92.6 1.1 %select_reduce_fusion.3 = (f32[768,4]{0,1:T(4,128)S(1)}, f32[768,4]{0,1:T(4,128)S(1)}) fusion(f32[768,4,360]{0,2,1:T(8,128)S(1)} %bitcast.47, pred[360]{0:T(512)(128)(4,1)S(1)} %get-tuple-element.152, pred[360]{0:T(512)(128)(4,1)S(1)} %get-tuple-element.153), kind=kLoop, calls=%fused_computation.2.clone.1 | loop fusion | flops 4417536 | bytes 4448976 | tf_op jit(solution)/shard_map/while/body/eval_jaxpr/reduce_max | solution.py:77
  93.8 1.1 %convolution_select_fusion.2 = f32[1440,768]{1,0:T(8,128)S(1)} fusion(bf16[768,128]{1,0:T(8,128)(2,1)S(1)} %get-tuple-element.172, pred[1440]{0:T(1024)(128)(4,1)S(1)} %compare_reduce_fusion.2, bf16[4,1440,128]{2,1,0:T(8,128)(2,1)S(1)} %get-tuple-element.171, s32[]{:T(128)} %get-tuple-element.162), kind=kOutput, calls=%fused_computation.3.clone.1 | convolution fusion | flops 284221440 | bytes 4990980 | tf_op jit(solution)/shard_map/while/body/eval_jaxpr/td,rd->tr/dot_general | solution.py:72
  95.0 1.1 %select_reduce_fusion.3 = (f32[768,4]{0,1:T(4,128)S(1)}, f32[768,4]{0,1:T(4,128)S(1)}) fusion(f32[768,4,360]{0,2,1:T(8,128)S(1)} %bitcast.47, pred[360]{0:T(512)(128)(4,1)S(1)} %get-tuple-element.152, pred[360]{0:T(512)(128)(4,1)S(1)} %get-tuple-element.153), kind=kLoop, calls=%fused_computation.2.clone.1 | loop fusion | flops 4417536 | bytes 4448976 | tf_op jit(solution)/shard_map/while/body/eval_jaxpr/reduce_max | solution.py:77
  96.6 0.7 copy.29
  (80 shorter events, 3.5 us)
Async XLA Ops:
  6.5 32.6 %copy-start = (bf16[24,32,768]{2,1,0:T(8,128)(2,1)S(1)}, bf16[24,32,768]{2,1,0:T(8,128)(2,1)}, u32[]{:S(2)}) copy-start(bf16[24,32,768]{2,1,0:T(8,128)(2,1)} %param.8) | copy-start | bytes 3538948
  6.5 78.3 %all-gather.5.cloned.1.call-start = ((), (), s32[]{:S(2)}) async-start(), calls=%async_computation | async-start | bytes 2211840 | tf_op jit(solution)/shard_map/all_gather | solution.py:62
  8.1 26.4 %copy-start.4 = (s32[2]{0:T(128)S(1)}, s32[2]{0:T(128)}, u32[]{:S(2)}) copy-start(s32[2]{0:T(128)} %param.12) | copy-start | bytes 28
  8.1 26.5 %copy-start.3 = (s32[1,180]{1,0:T(1,128)S(1)}, s32[1,180]{1,0:T(1,128)}, u32[]{:S(2)}) copy-start(s32[1,180]{1,0:T(1,128)} %param.11) | copy-start | bytes 2164
  33.5 5.6 %copy-start.1 = (bf16[768,128]{1,0:T(8,128)(2,1)S(1)}, bf16[768,128]{1,0:T(8,128)(2,1)}, u32[]{:S(2)}) copy-start(bf16[768,128]{1,0:T(8,128)(2,1)} %param.13) | copy-start | bytes 589828
  34.6 5.7 %collective-permute-start = (bf16[1,180]{1,0:T(2,128)(2,1)S(1)}, bf16[1,180]{1,0:T(2,128)(2,1)S(1)}, u32[]{:S(2)}, u32[]{:S(2)}) collective-permute-start(bf16[1,180]{1,0:T(2,128)(2,1)S(1)} %and_convert_fusion), channel_id=1, source_target_pairs={{0,1},{1,2},{2,3},{3,4},{4,5},{5,6},{6,7},{7,8},{8,9},{9,10},{10,1... | collective-permute-start | bytes 1088 | tf_op jit(solution)/shard_map/ppermute | solution.py:23
  35.0 5.5 %collective-permute-start.1 = (bf16[1,180]{1,0:T(2,128)(2,1)S(1)}, bf16[1,180]{1,0:T(2,128)(2,1)S(1)}, u32[]{:S(2)}, u32[]{:S(2)}) collective-permute-start(bf16[1,180]{1,0:T(2,128)(2,1)S(1)} %and_convert_fusion), channel_id=1, source_target_pairs={{0,15},{1,0},{2,1},{3,2},{4,3},{5,4},{6,5},{7,6},{8,7},{9,8},{10,9... | collective-permute-start | bytes 1088 | tf_op jit(solution)/shard_map/ppermute | solution.py:26
  39.1 1.4 %copy-start.2 = (s32[24,32]{1,0:T(8,128)S(1)}, s32[24,32]{1,0:T(8,128)}, u32[]{:S(2)}) copy-start(s32[24,32]{1,0:T(8,128)} %param.9) | copy-start | bytes 9220
  40.4 5.7 %collective-permute-start.2 = (bf16[1,180]{1,0:T(2,128)(2,1)S(1)}, bf16[1,180]{1,0:T(2,128)(2,1)S(1)}, u32[]{:S(2)}, u32[]{:S(2)}) collective-permute-start(bf16[1,180]{1,0:T(2,128)(2,1)S(1)} %collective-permute-done), channel_id=1, source_target_pairs={{0,1},{1,2},{2,3},{3,4},{4,5},{5,6},{6,7},{7,8},{8,9},{9,10},{10,1... | collective-permute-start | bytes 1088 | tf_op jit(solution)/shard_map/ppermute | solution.py:23
  40.6 5.8 %collective-permute-start.3 = (bf16[1,180]{1,0:T(2,128)(2,1)S(1)}, bf16[1,180]{1,0:T(2,128)(2,1)S(1)}, u32[]{:S(2)}, u32[]{:S(2)}) collective-permute-start(bf16[1,180]{1,0:T(2,128)(2,1)S(1)} %collective-permute-done.1), channel_id=1, source_target_pairs={{0,15},{1,0},{2,1},{3,2},{4,3},{5,4},{6,5},{7,6},{8,7},{9,8},{10,9... | collective-permute-start | bytes 1088 | tf_op jit(solution)/shard_map/ppermute | solution.py:26
  46.1 5.7 %collective-permute-start.4 = (bf16[1,180]{1,0:T(2,128)(2,1)S(1)}, bf16[1,180]{1,0:T(2,128)(2,1)S(1)}, u32[]{:S(2)}, u32[]{:S(2)}) collective-permute-start(bf16[1,180]{1,0:T(2,128)(2,1)S(1)} %collective-permute-done.2), channel_id=1, source_target_pairs={{0,1},{1,2},{2,3},{3,4},{4,5},{5,6},{6,7},{7,8},{8,9},{9,10},{10,1... | collective-permute-start | bytes 1088 | tf_op jit(solution)/shard_map/ppermute | solution.py:23
  46.4 5.7 %collective-permute-start.5 = (bf16[1,180]{1,0:T(2,128)(2,1)S(1)}, bf16[1,180]{1,0:T(2,128)(2,1)S(1)}, u32[]{:S(2)}, u32[]{:S(2)}) collective-permute-start(bf16[1,180]{1,0:T(2,128)(2,1)S(1)} %collective-permute-done.3), channel_id=1, source_target_pairs={{0,15},{1,0},{2,1},{3,2},{4,3},{5,4},{6,5},{7,6},{8,7},{9,8},{10,9... | collective-permute-start | bytes 1088 | tf_op jit(solution)/shard_map/ppermute | solution.py:26
  51.8 5.7 %collective-permute-start.6 = (bf16[1,180]{1,0:T(2,128)(2,1)S(1)}, bf16[1,180]{1,0:T(2,128)(2,1)S(1)}, u32[]{:S(2)}, u32[]{:S(2)}) collective-permute-start(bf16[1,180]{1,0:T(2,128)(2,1)S(1)} %collective-permute-done.4), channel_id=1, source_target_pairs={{0,1},{1,2},{2,3},{3,4},{4,5},{5,6},{6,7},{7,8},{8,9},{9,10},{10,1... | collective-permute-start | bytes 1088 | tf_op jit(solution)/shard_map/ppermute | solution.py:23
  52.1 5.7 %collective-permute-start.7 = (bf16[1,180]{1,0:T(2,128)(2,1)S(1)}, bf16[1,180]{1,0:T(2,128)(2,1)S(1)}, u32[]{:S(2)}, u32[]{:S(2)}) collective-permute-start(bf16[1,180]{1,0:T(2,128)(2,1)S(1)} %collective-permute-done.5), channel_id=1, source_target_pairs={{0,15},{1,0},{2,1},{3,2},{4,3},{5,4},{6,5},{7,6},{8,7},{9,8},{10,9... | collective-permute-start | bytes 1088 | tf_op jit(solution)/shard_map/ppermute | solution.py:26
  57.4 5.7 %collective-permute-start.8 = (bf16[1,180]{1,0:T(2,128)(2,1)S(1)}, bf16[1,180]{1,0:T(2,128)(2,1)S(1)}, u32[]{:S(2)}, u32[]{:S(2)}) collective-permute-start(bf16[1,180]{1,0:T(2,128)(2,1)S(1)} %collective-permute-done.6), channel_id=1, source_target_pairs={{0,1},{1,2},{2,3},{3,4},{4,5},{5,6},{6,7},{7,8},{8,9},{9,10},{10,1... | collective-permute-start | bytes 1088 | tf_op jit(solution)/shard_map/ppermute | solution.py:23
  57.8 5.7 %collective-permute-start.9 = (bf16[1,180]{1,0:T(2,128)(2,1)S(1)}, bf16[1,180]{1,0:T(2,128)(2,1)S(1)}, u32[]{:S(2)}, u32[]{:S(2)}) collective-permute-start(bf16[1,180]{1,0:T(2,128)(2,1)S(1)} %collective-permute-done.7), channel_id=1, source_target_pairs={{0,15},{1,0},{2,1},{3,2},{4,3},{5,4},{6,5},{7,6},{8,7},{9,8},{10,9... | collective-permute-start | bytes 1088 | tf_op jit(solution)/shard_map/ppermute | solution.py:26
  63.1 5.7 %collective-permute-start.10 = (bf16[1,180]{1,0:T(2,128)(2,1)S(1)}, bf16[1,180]{1,0:T(2,128)(2,1)S(1)}, u32[]{:S(2)}, u32[]{:S(2)}) collective-permute-start(bf16[1,180]{1,0:T(2,128)(2,1)S(1)} %collective-permute-done.8), channel_id=1, source_target_pairs={{0,1},{1,2},{2,3},{3,4},{4,5},{5,6},{6,7},{7,8},{8,9},{9,10},{10,1... | collective-permute-start | bytes 1088 | tf_op jit(solution)/shard_map/ppermute | solution.py:23
  63.5 5.7 %collective-permute-start.11 = (bf16[1,180]{1,0:T(2,128)(2,1)S(1)}, bf16[1,180]{1,0:T(2,128)(2,1)S(1)}, u32[]{:S(2)}, u32[]{:S(2)}) collective-permute-start(bf16[1,180]{1,0:T(2,128)(2,1)S(1)} %collective-permute-done.9), channel_id=1, source_target_pairs={{0,15},{1,0},{2,1},{3,2},{4,3},{5,4},{6,5},{7,6},{8,7},{9,8},{10,9... | collective-permute-start | bytes 1088 | tf_op jit(solution)/shard_map/ppermute | solution.py:26
  68.8 5.7 %collective-permute-start.12 = (bf16[1,180]{1,0:T(2,128)(2,1)S(1)}, bf16[1,180]{1,0:T(2,128)(2,1)S(1)}, u32[]{:S(2)}, u32[]{:S(2)}) collective-permute-start(bf16[1,180]{1,0:T(2,128)(2,1)S(1)} %collective-permute-done.10), channel_id=1, source_target_pairs={{0,1},{1,2},{2,3},{3,4},{4,5},{5,6},{6,7},{7,8},{8,9},{9,10},{10,1... | collective-permute-start | bytes 1088 | tf_op jit(solution)/shard_map/ppermute | solution.py:23
  69.1 5.7 %collective-permute-start.13 = (bf16[1,180]{1,0:T(2,128)(2,1)S(1)}, bf16[1,180]{1,0:T(2,128)(2,1)S(1)}, u32[]{:S(2)}, u32[]{:S(2)}) collective-permute-start(bf16[1,180]{1,0:T(2,128)(2,1)S(1)} %collective-permute-done.11), channel_id=1, source_target_pairs={{0,15},{1,0},{2,1},{3,2},{4,3},{5,4},{6,5},{7,6},{8,7},{9,8},{10,9... | collective-permute-start | bytes 1088 | tf_op jit(solution)/shard_map/ppermute | solution.py:26
  74.5 5.7 %collective-permute-start.14 = (bf16[1,180]{1,0:T(2,128)(2,1)S(1)}, bf16[1,180]{1,0:T(2,128)(2,1)S(1)}, u32[]{:S(2)}, u32[]{:S(2)}) collective-permute-start(bf16[1,180]{1,0:T(2,128)(2,1)S(1)} %collective-permute-done.12), channel_id=1, source_target_pairs={{0,1},{1,2},{2,3},{3,4},{4,5},{5,6},{6,7},{7,8},{8,9},{9,10},{10,1... | collective-permute-start | bytes 1088 | tf_op jit(solution)/shard_map/ppermute | solution.py:23
Sparse Core Ops, SparseCore 0:
  34.6 23.3 all-gather.4
